TPU v7x, 128 devices: a whole 4x4x4 slice. The times are simulated.
128 devices in a mesh: tm: 32 (over z, y, x_lo), slab: 4 (over x_hi, core).
Axes of the slice: x: 4 (x_hi: 2, x_lo: 2; x = x_hi * 2 + x_lo), y: 4, z: 4, core: 2. Of those that a mesh axis runs over, the one named last changes fastest.
Arguments:
- kspace: bfloat16 [2, 64, 4, 96, 9984], P(None, 'tm', None, 'slab'), may hold values from -40 to 40, as said below
- sens: float32 [2, 4, 8, 104, 96], P(None, None, None, 'slab'), may hold values from -3 to 3
Outputs:
- projected: float32 [64, 2, 8, 104, 96], P('tm', None, None, 'slab')
Inputs may be any that keep to these rules, and one draw needn't show every extreme that they name: `kspace`: k-space values of order one with frames of different scale.
All inputs are finite; a program needn't handle non-finite values.
Results may differ from a plain program's by a relative error of at most 0.0036.
Values may be sent and summed in bfloat16 or wider, within the bound.
A program may use at most 128 MiB of HBM per device.

v0:
```python
import jax
import jax.numpy as jnp
from jax import lax
from jax.sharding import PartitionSpec as P

NX = 96
NY = 104
NZ = 96
RANK = 32
ITERS = 4
XW = 8


def inverse_table(length, count, offset):
    outputs = jnp.arange(count, dtype=jnp.int32) + offset
    inputs = jnp.arange(length, dtype=jnp.int32)
    phase = outputs[:, None] * inputs[None, :] % length
    angle = phase.astype(jnp.float32) * (2.0 * jnp.pi / length)
    norm_factor = 1.0 / jnp.sqrt(jnp.float32(length))
    return (jnp.cos(angle) * norm_factor, jnp.sin(angle) * norm_factor)


def contract(pattern, matrix_table, operand):
    return jnp.einsum(pattern, matrix_table, operand, precision=lax.Precision.HIGHEST)


def matmul(left, right):
    return jnp.dot(left, right, precision=lax.Precision.HIGHEST)


def orthonormal(rows, gram):
    factor = jnp.linalg.cholesky(matmul(matmul(rows, gram), rows.T))
    return lax.linalg.triangular_solve(factor, rows, left_side=True, lower=True)


def local(kspace, sens):
    frames_dev = kspace.shape[1]
    coil_count = kspace.shape[2]
    depth_dev = kspace.shape[3]
    spectrum = kspace.astype(jnp.float32).reshape(2, frames_dev, coil_count, depth_dev, NX, NY)
    across_cos, across_sin = inverse_table(NX, XW, (NX - XW) // 2)
    down_cos, down_sin = inverse_table(NY, NY, 0)
    depth_cos, depth_sin = inverse_table(NZ, NZ, 0)
    across_real = contract("jx,fczxy->fczjy", across_cos, spectrum[0]) - contract(
        "jx,fczxy->fczjy", across_sin, spectrum[1]
    )
    across_other = contract("jx,fczxy->fczjy", across_cos, spectrum[1]) + contract(
        "jx,fczxy->fczjy", across_sin, spectrum[0]
    )
    down_real = contract("my,fczjy->fczjm", down_cos, across_real) - contract(
        "my,fczjy->fczjm", down_sin, across_other
    )
    down_other = contract("my,fczjy->fczjm", down_cos, across_other) + contract(
        "my,fczjy->fczjm", down_sin, across_real
    )
    planes = jnp.stack([down_real, down_other]).astype(jnp.bfloat16)
    arrived = lax.all_to_all(planes, "slab", split_axis=5, concat_axis=3, tiled=True).astype(
        jnp.float32
    )
    depth_real = contract("wz,fczxy->fcxyw", depth_cos, arrived[0]) - contract(
        "wz,fczxy->fcxyw", depth_sin, arrived[1]
    )
    depth_other = contract("wz,fczxy->fcxyw", depth_cos, arrived[1]) + contract(
        "wz,fczxy->fcxyw", depth_sin, arrived[0]
    )
    sens_real = sens[0][None]
    sens_other = sens[1][None]
    combined_real = jnp.sum(sens_real * depth_real + sens_other * depth_other, axis=1)
    combined_other = jnp.sum(sens_real * depth_other - sens_other * depth_real, axis=1)
    matrix = jnp.stack([combined_real, combined_other], axis=1).reshape(frames_dev, -1)
    rows = lax.all_to_all(matrix, "tm", split_axis=1, concat_axis=0, tiled=True)
    gram = lax.psum(matmul(rows, rows.T), ("tm", "slab"))
    eye = jnp.eye(RANK, dtype=jnp.float32)
    current = jnp.concatenate([eye, eye], axis=1)
    for sweep_index in range(ITERS):
        current = matmul(orthonormal(current, gram), gram)
    coeff = orthonormal(current, gram)
    mixing = matmul(matmul(coeff, gram).T, coeff)
    projected = matmul(mixing, rows)
    projected = lax.all_to_all(projected, "tm", split_axis=0, concat_axis=1, tiled=True)
    return projected.reshape(frames_dev, 2, XW, -1, NZ)


def solution(mesh):
    in_specs = (P(None, "tm", None, "slab", None), P(None, None, None, "slab", None))
    out_specs = P("tm", None, None, "slab", None)
    return jax.shard_map(local, mesh=mesh, in_specs=in_specs, out_specs=out_specs, check_vma=False)
```

profile of v0, /device:TPU:0, one launch (start us, length us, event | category | flops | bytes accessed | tf_op | source)
XLA Modules:
  0.0 234.5 jit_solution(5598859404871233806)
XLA Ops:
  0.0 5.4 %fusion.180 = (bf16[1,2,4,24,9984]{4,3,2,1,0:T(8,128)(2,1)}, bf16[1,2,4,24,9984]{4,3,2,1,0:T(8,128)(2,1)}) fusion(bf16[2,2,4,24,9984]{4,3,2,1,0:T(8,128)(2,1)} %param.5), kind=kLoop, calls=%fused_computation.213 | loop fusion | bytes 15335424 | tf_op jit(solution)/shard_map/slice | solution.py:44
  5.4 13.7 %squeeze.16 = bf16[2,4,24,96,104]{4,3,2,1,0:T(8,128)(2,1)} reshape(bf16[1,2,4,24,9984]{4,3,2,1,0:T(8,128)(2,1)} %get-tuple-element.9) | data formatting | bytes 7667712 | tf_op jit(solution)/shard_map/squeeze | solution.py:44
  19.2 13.8 %squeeze.17 = bf16[2,4,24,96,104]{4,3,2,1,0:T(8,128)(2,1)} reshape(bf16[1,2,4,24,9984]{4,3,2,1,0:T(8,128)(2,1)} %get-tuple-element.10) | data formatting | bytes 7667712 | tf_op jit(solution)/shard_map/squeeze | solution.py:45
  33.0 4.3 %fusion.105 = f32[8,2,4,24,104]{4,0,3,2,1:T(8,128)S(1)} fusion(bf16[2,4,24,96,104]{4,3,2,1,0:T(8,128)(2,1)} %squeeze.16, s32[8]{0:T(128)S(1)} %iota_add_fusion), kind=kOutput, calls=%fused_computation.133 | convolution fusion | flops 184032768 | bytes 4472864 | tf_op jit(solution)/shard_map/jx,fczxy->fczjy/dot_general | solution.py:24
  37.3 2.1 fusion.103
  39.4 2.1 fusion.1
  41.4 1.0 fusion.10
  42.5 2.1 fusion
  44.5 1.0 fusion.6
  45.5 1.0 fusion.5
  46.5 1.0 fusion.4
  47.5 1.1 pad_maximum_fusion
  48.6 5.8 %copy.42 = bf16[2,2,4,24,8,104]{3,4,2,1,0,5:T(8,128)(2,1)S(1)} copy(bf16[2,2,4,24,8,104]{5,3,4,2,1,0:T(8,128)(2,1)} %pad_maximum_fusion) | data formatting | bytes 1277952 | tf_op jit(solution)/shard_map/stack | solution.py:56
  54.4 5.0 %reshape.64 = bf16[4,2,39936]{2,1,0:T(2,128)(2,1)} reshape(bf16[104,2,2,4,8,24]{5,4,3,2,1,0:T(8,128)(2,1)S(1)} %bitcast.164) | data formatting | bytes 1277952
  59.4 4.4 %all-to-all-start = ((bf16[4,2,39936]{2,1,0:T(2,128)(2,1)}), bf16[4,2,39936]{2,1,0:T(2,128)(2,1)}, u32[]{:S(2)}, u32[]{:S(2)}) async-start(bf16[4,2,39936]{2,1,0:T(2,128)(2,1)} %reshape.64), calls=%async_computation | async-start | bytes 1277952 | tf_op jit(solution)/shard_map/all_to_all | solution.py:57
  63.8 1.2 slice_bitcast_fusion.1
  65.0 0.9 copy.37
  65.9 0.9 copy.46
  66.8 8.7 %all-to-all-done = bf16[4,2,39936]{2,1,0:T(2,128)(2,1)} async-done(((bf16[4,2,39936]{2,1,0:T(2,128)(2,1)}), bf16[4,2,39936]{2,1,0:T(2,128)(2,1)}, u32[]{:S(2)}, u32[]{:S(2)}) %all-to-all-start) | async-done | bytes 639008 | tf_op jit(solution)/shard_map/all_to_all | solution.py:57
  75.5 5.6 %reshape.65 = bf16[104,2,2,4,8,24]{5,4,3,2,1,0:T(8,128)(2,1)S(1)} reshape(bf16[4,2,39936]{2,1,0:T(2,128)(2,1)} %all-to-all-done) | data formatting | bytes 1277952
  81.1 4.4 %copy.86 = bf16[2,2,4,24,8,4,26]{3,5,4,6,2,1,0:T(4,128)(2,1)S(1)} copy(bf16[2,2,4,24,8,4,26]{3,4,2,1,0,6,5:T(8,128)(2,1)S(1)} %bitcast.165) | data formatting | bytes 1277952 | tf_op jit(solution)/shard_map/all_to_all | solution.py:57
  85.5 1.2 fusion.181
  86.7 1.6 squeeze.18
  88.3 2.9 %fusion.16 = f32[2,4,8,26,96]{4,3,2,1,0:T(8,128)} fusion(bf16[2,4,96,8,26]{2,3,4,1,0:T(8,128)(2,1)} %squeeze.18), kind=kOutput, calls=%fused_computation.27 | convolution fusion | flops 184117248 | bytes 958464 | tf_op jit(solution)/shard_map/wz,fczxy->fcxyw/dot_general | solution.py:24
  91.1 0.9 squeeze.19
  92.0 0.8 fusion.12
  92.8 2.0 convolution_subtract_fusion
  94.9 2.2 add_reduce_fusion
  97.3 1.0 copy.49
  98.3 9.4 %all-to-all-start.1 = ((f32[2,32,1248]{2,0,1:T(2,128)}), f32[2,32,1248]{2,0,1:T(2,128)S(1)}, u32[]{:S(2)}, u32[]{:S(2)}) async-start(f32[2,32,1248]{2,0,1:T(2,128)} %copy.49), calls=%async_computation.1 | async-start | bytes 655360 | tf_op jit(solution)/shard_map/all_to_all | solution.py:71
  107.7 9.6 %all-to-all-done.1 = f32[2,32,1248]{2,0,1:T(2,128)S(1)} async-done(((f32[2,32,1248]{2,0,1:T(2,128)}), f32[2,32,1248]{2,0,1:T(2,128)S(1)}, u32[]{:S(2)}, u32[]{:S(2)}) %all-to-all-start.1) | async-done | bytes 319520 | tf_op jit(solution)/shard_map/all_to_all | solution.py:71
  117.8 0.4 fusion.182
  118.2 62.4 %psum.7 = f32[64,64]{1,0:T(8,128)S(1)} all-reduce(f32[64,64]{1,0:T(8,128)S(1)} %fusion.182), channel_id=1, replica_groups=mesh['tm'=32,'slab'=4] {'tm','slab'}, use_global_device_ids=true, to_apply=%region_2.3 | all-reduce | flops 4096 | bytes 32768 | tf_op jit(solution)/shard_map/psum | solution.py:72
  181.1 2.9 %cholesky.89 = f32[32,32]{1,0:T(8,128)S(1)} custom-call(f32[32,32]{1,0:T(8,128)S(1)} %fusion.89), custom_call_target="Cholesky" | custom-call | tf_op jit(solution)/shard_map/jit(cholesky)/cholesky | solution.py:32
  184.1 0.6 compare_reduce_fusion.4
  184.7 0.7 fusion.70
  185.4 2.4 %custom-call.9 = f32[1,32,32]{1,2,0:T(8,128)S(1)} custom-call(f32[1,32,32]{2,1,0:T(8,128)S(1)} %fusion.70), custom_call_target="InvertDiagBlocksLowerTriangular" | custom-call | tf_op jit(solution)/shard_map/triangular_solve/custom-call.0 | solution.py:33
  187.8 0.3 fusion.87
  188.6 2.9 %cholesky.100 = f32[32,32]{1,0:T(8,128)S(1)} custom-call(f32[32,32]{1,0:T(8,128)S(1)} %fusion.86), custom_call_target="Cholesky" | custom-call | tf_op jit(solution)/shard_map/jit(cholesky)/cholesky | solution.py:32
  191.6 0.6 compare_reduce_fusion.3
  192.2 0.7 fusion.71
  192.9 2.4 %custom-call.10 = f32[1,32,32]{1,2,0:T(8,128)S(1)} custom-call(f32[1,32,32]{2,1,0:T(8,128)S(1)} %fusion.71), custom_call_target="InvertDiagBlocksLowerTriangular" | custom-call | tf_op jit(solution)/shard_map/triangular_solve/custom-call.0 | solution.py:33
  195.3 0.2 fusion.84
  196.1 2.9 %cholesky.111 = f32[32,32]{1,0:T(8,128)S(1)} custom-call(f32[32,32]{1,0:T(8,128)S(1)} %fusion.83), custom_call_target="Cholesky" | custom-call | tf_op jit(solution)/shard_map/jit(cholesky)/cholesky | solution.py:32
  199.1 0.6 compare_reduce_fusion.2
  199.7 0.7 fusion.72
  200.4 2.4 %custom-call.11 = f32[1,32,32]{1,2,0:T(8,128)S(1)} custom-call(f32[1,32,32]{2,1,0:T(8,128)S(1)} %fusion.72), custom_call_target="InvertDiagBlocksLowerTriangular" | custom-call | tf_op jit(solution)/shard_map/triangular_solve/custom-call.0 | solution.py:33
  202.8 0.2 fusion.81
  203.6 2.9 %cholesky.122 = f32[32,32]{1,0:T(8,128)S(1)} custom-call(f32[32,32]{1,0:T(8,128)S(1)} %fusion.80), custom_call_target="Cholesky" | custom-call | tf_op jit(solution)/shard_map/jit(cholesky)/cholesky | solution.py:32
  206.5 0.6 compare_reduce_fusion.1
  207.2 0.7 fusion.73
  207.8 2.4 %custom-call.12 = f32[1,32,32]{1,2,0:T(8,128)S(1)} custom-call(f32[1,32,32]{2,1,0:T(8,128)S(1)} %fusion.73), custom_call_target="InvertDiagBlocksLowerTriangular" | custom-call | tf_op jit(solution)/shard_map/triangular_solve/custom-call.0 | solution.py:33
  210.3 0.2 fusion.78
  211.1 2.9 %cholesky.133 = f32[32,32]{1,0:T(8,128)S(1)} custom-call(f32[32,32]{1,0:T(8,128)S(1)} %fusion.77), custom_call_target="Cholesky" | custom-call | tf_op jit(solution)/shard_map/jit(cholesky)/cholesky | solution.py:32
  214.0 0.6 compare_reduce_fusion
  214.7 0.7 fusion.74
  215.3 2.4 %custom-call.13 = f32[1,32,32]{1,2,0:T(8,128)S(1)} custom-call(f32[1,32,32]{2,1,0:T(8,128)S(1)} %fusion.74), custom_call_target="InvertDiagBlocksLowerTriangular" | custom-call | tf_op jit(solution)/shard_map/triangular_solve/custom-call.0 | solution.py:33
  217.8 0.2 fusion.75
  218.2 0.2 fusion.196
  218.4 0.4 fusion.36
  218.8 0.3 copy.56
  219.1 14.0 %all_to_all.47 = f32[32,2,1248]{2,1,0:T(2,128)S(1)} all-to-all(f32[32,2,1248]{2,1,0:T(2,128)S(1)} %copy.56), channel_id=1, replica_groups=mesh['tm'=32,'slab'=4] {'tm'}, dimensions={0} | all-to-all | bytes 638976 | tf_op jit(solution)/shard_map/all_to_all | solution.py:80
  233.2 0.3 reshape.37
  233.4 1.0 copy.58
  (48 shorter events, 3.6 us)
Async XLA Ops:
  33.0 4.3 %copy-start = (bf16[2,4,24,96,104]{4,3,2,1,0:T(8,128)(2,1)S(1)}, bf16[2,4,24,96,104]{4,3,2,1,0:T(8,128)(2,1)}, u32[]{:S(2)}) copy-start(bf16[2,4,24,96,104]{4,3,2,1,0:T(8,128)(2,1)} %squeeze.17) | copy-start | bytes 11501572
  37.3 5.1 %slice-start = ((s8[4718592]{0:T(1024)(128)(4,1)}), s8[4194304]{0:T(1024)(128)(4,1)S(1)}, s32[]{:S(2)}) async-start(s8[4718592]{0:T(1024)(128)(4,1)} %bitcast.161), calls=%async_computation.3 | async-start | bytes 8388608
  39.4 3.1 %slice-start.1 = ((s8[4718592]{0:T(1024)(128)(4,1)}), s8[524288]{0:T(1024)(128)(4,1)S(1)}, s32[]{:S(2)}) async-start(s8[4718592]{0:T(1024)(128)(4,1)} %bitcast.161), calls=%async_computation.4 | async-start | bytes 1048576
  59.4 16.1 %all-to-all-start = ((bf16[4,2,39936]{2,1,0:T(2,128)(2,1)}), bf16[4,2,39936]{2,1,0:T(2,128)(2,1)}, u32[]{:S(2)}, u32[]{:S(2)}) async-start(bf16[4,2,39936]{2,1,0:T(2,128)(2,1)} %reshape.64), calls=%async_computation | async-start | bytes 1277952 | tf_op jit(solution)/shard_map/all_to_all | solution.py:57
  88.3 6.6 %copy-start.1 = (bf16[2,4,96,8,26]{2,3,4,1,0:T(8,128)(2,1)S(1)}, bf16[2,4,96,8,26]{2,3,4,1,0:T(8,128)(2,1)}, u32[]{:S(2)}) copy-start(bf16[2,4,96,8,26]{2,3,4,1,0:T(8,128)(2,1)} %squeeze.18) | copy-start | bytes 958468
  88.3 6.6 %copy-start.2 = (f32[4,8,26,96]{3,2,1,0:T(8,128)S(1)}, f32[4,8,26,96]{3,2,1,0:T(8,128)}, u32[]{:S(2)}) copy-start(f32[4,8,26,96]{3,2,1,0:T(8,128)} %copy.37) | copy-start | bytes 958468
  98.3 19.0 %all-to-all-start.1 = ((f32[2,32,1248]{2,0,1:T(2,128)}), f32[2,32,1248]{2,0,1:T(2,128)S(1)}, u32[]{:S(2)}, u32[]{:S(2)}) async-start(f32[2,32,1248]{2,0,1:T(2,128)} %copy.49), calls=%async_computation.1 | async-start | bytes 655360 | tf_op jit(solution)/shard_map/all_to_all | solution.py:71
where the time goes:
time: 235 us; the launch traced here: 234 us
  blocking collectives  76.4 us (33%)
  local copies, waits for them, and re-layouts  64.1 us (27%)
  other arithmetic  34.6 us (15%)
  matrix products  26.8 us (11%)
  waiting for transfers between devices  18.3 us (8%)
  starting transfers between devices  13.7 us (6%)
    psum x1, blocking collectives, local(): gram = lax.psum(matmul(rows, rows.T), ('tm', 'slab'))  62.4 us
    dot_general x12, matrix products, contract(): jnp.einsum(pattern, matrix_table, operand, precision=lax.Precision.HIGHEST)  22.3 us
    another operation x16, other arithmetic, orthonormal(): factor = jnp.linalg.cholesky(matmul(matmul(rows, gram), rows.T))  18 us
    another operation x10, other arithmetic, orthonormal(): return lax.linalg.triangular_solve(factor, rows, left_side=True, lower=True)  15.4 us
    all_to_all x1, blocking collectives, local(): lax.all_to_all(projected, 'tm', split_axis=0, concat_axis=1, tiled=True)  14 us
    squeeze x1, local copies, waits for them, and re-layouts, local(): spectrum[1]  13.8 us
    squeeze x1, local copies, waits for them, and re-layouts, local(): spectrum[0]  13.7 us
    unnamed x12, local copies, waits for them, and re-layouts  10.6 us
  transfers between devices with their start and end apart: 2, of which 2 were waited for; matrix products, arithmetic and copies ran while one was open for 1% of the time, Pallas kernels for 0%

commit v1 on v0

--- a/solution.py
+++ b/solution.py
@@ -69,7 +69,7 @@
     combined_other = jnp.sum(sens_real * depth_other - sens_other * depth_real, axis=1)
     matrix = jnp.stack([combined_real, combined_other], axis=1).reshape(frames_dev, -1)
     rows = lax.all_to_all(matrix, "tm", split_axis=1, concat_axis=0, tiled=True)
-    gram = lax.psum(matmul(rows, rows.T), ("tm", "slab"))
+    gram = jnp.sum(lax.all_gather(matmul(rows, rows.T), ("tm", "slab")), axis=0)
     eye = jnp.eye(RANK, dtype=jnp.float32)
     current = jnp.concatenate([eye, eye], axis=1)
     for sweep_index in range(ITERS):

time: 235 us -> 383 us (1.63)
  waiting for transfers between devices: 18.3 us -> 203 us
  blocking collectives: 76.4 us -> 34.1 us
  between operations: 0.48 us -> 13.9 us
  starting transfers between devices: 13.7 us -> 4.38 us
    all_gather x0 -> x1, waiting for transfers between devices: none -> 194 us  [local(): gram = jnp.sum(lax.all_gather(matmul(rows, rows.T), ('tm', 'slab')), axis=0)]
    psum x1 -> x0, blocking collectives: 62.4 us -> none  [local(): gram = lax.psum(matmul(rows, rows.T), ('tm', 'slab'))]
    all_to_all x0 -> x1, blocking collectives: none -> 18.8 us  [local(): rows = lax.all_to_all(matrix, 'tm', split_axis=1, concat_axis=0, tiled=True)]
    all_to_all x1 -> x0, waiting for transfers between devices: 9.63 us -> none  [local(): rows = lax.all_to_all(matrix, 'tm', split_axis=1, concat_axis=0, tiled=True)]
    all_to_all x1 -> x0, starting transfers between devices: 9.35 us -> none  [local(): rows = lax.all_to_all(matrix, 'tm', split_axis=1, concat_axis=0, tiled=True)]
where the time goes in v1:
time: 383 us
  waiting for transfers between devices  203 us (53%)
  local copies, waits for them, and re-layouts  63.4 us (17%)
  other arithmetic  37.1 us (10%)
  blocking collectives  34.1 us (9%)
  matrix products  27.4 us (7%)
  between operations  13.9 us (4%)
  starting transfers between devices  4.38 us (1%)
    all_gather x1, waiting for transfers between devices, local(): gram = jnp.sum(lax.all_gather(matmul(rows, rows.T), ('tm', 'slab')), axis=0)  194 us
    dot_general x12, matrix products, contract(): jnp.einsum(pattern, matrix_table, operand, precision=lax.Precision.HIGHEST)  22.3 us
    all_to_all x1, blocking collectives, local(): rows = lax.all_to_all(matrix, 'tm', split_axis=1, concat_axis=0, tiled=True)  18.8 us
    another operation x16, other arithmetic, orthonormal(): factor = jnp.linalg.cholesky(matmul(matmul(rows, gram), rows.T))  18 us
    another operation x10, other arithmetic, orthonormal(): return lax.linalg.triangular_solve(factor, rows, left_side=True, lower=True)  15.4 us
    all_to_all x1, blocking collectives, local(): lax.all_to_all(projected, 'tm', split_axis=0, concat_axis=1, tiled=True)  15.2 us
    squeeze x1, local copies, waits for them, and re-layouts, local(): spectrum[1]  13.8 us
    squeeze x1, local copies, waits for them, and re-layouts, local(): spectrum[0]  13.7 us
  transfers between devices with their start and end apart: 2, of which 2 were waited for; matrix products, arithmetic and copies ran while one was open for 1% of the time, Pallas kernels for 0%

profile of v1, /device:TPU:0, one launch (start us, length us, event | category | flops | bytes accessed | tf_op | source)
XLA Modules:
  0.0 382.8 jit_solution(10691633709992010446)
XLA Ops:
  6.5 5.4 %fusion.180 = (bf16[1,2,4,24,9984]{4,3,2,1,0:T(8,128)(2,1)}, bf16[1,2,4,24,9984]{4,3,2,1,0:T(8,128)(2,1)}) fusion(bf16[2,2,4,24,9984]{4,3,2,1,0:T(8,128)(2,1)} %param.5), kind=kLoop, calls=%fused_computation.213 | loop fusion | bytes 15335424 | tf_op jit(solution)/shard_map/slice | solution.py:44
  12.0 13.7 %squeeze.16 = bf16[2,4,24,96,104]{4,3,2,1,0:T(8,128)(2,1)} reshape(bf16[1,2,4,24,9984]{4,3,2,1,0:T(8,128)(2,1)} %get-tuple-element.9) | data formatting | bytes 7667712 | tf_op jit(solution)/shard_map/squeeze | solution.py:44
  25.7 13.8 %squeeze.17 = bf16[2,4,24,96,104]{4,3,2,1,0:T(8,128)(2,1)} reshape(bf16[1,2,4,24,9984]{4,3,2,1,0:T(8,128)(2,1)} %get-tuple-element.10) | data formatting | bytes 7667712 | tf_op jit(solution)/shard_map/squeeze | solution.py:45
  39.6 4.3 %fusion.105 = f32[8,2,4,24,104]{4,0,3,2,1:T(8,128)S(1)} fusion(bf16[2,4,24,96,104]{4,3,2,1,0:T(8,128)(2,1)} %squeeze.16, s32[8]{0:T(128)S(1)} %iota_add_fusion), kind=kOutput, calls=%fused_computation.133 | convolution fusion | flops 184032768 | bytes 4472864 | tf_op jit(solution)/shard_map/jx,fczxy->fczjy/dot_general | solution.py:24
  43.9 2.1 fusion.103
  45.9 2.1 fusion.1
  48.0 1.0 fusion.10
  49.0 2.1 fusion
  51.1 1.0 fusion.6
  52.1 1.0 fusion.5
  53.1 1.0 fusion.4
  54.1 1.1 pad_maximum_fusion
  55.1 5.8 %copy.42 = bf16[2,2,4,24,8,104]{3,4,2,1,0,5:T(8,128)(2,1)S(1)} copy(bf16[2,2,4,24,8,104]{5,3,4,2,1,0:T(8,128)(2,1)} %pad_maximum_fusion) | data formatting | bytes 1277952 | tf_op jit(solution)/shard_map/stack | solution.py:56
  60.9 5.0 %reshape.65 = bf16[4,2,39936]{2,1,0:T(2,128)(2,1)} reshape(bf16[104,2,2,4,8,24]{5,4,3,2,1,0:T(8,128)(2,1)S(1)} %bitcast.165) | data formatting | bytes 1277952
  65.9 4.4 %all-to-all-start = ((bf16[4,2,39936]{2,1,0:T(2,128)(2,1)}), bf16[4,2,39936]{2,1,0:T(2,128)(2,1)}, u32[]{:S(2)}, u32[]{:S(2)}) async-start(bf16[4,2,39936]{2,1,0:T(2,128)(2,1)} %reshape.65), calls=%async_computation | async-start | bytes 1277952 | tf_op jit(solution)/shard_map/all_to_all | solution.py:57
  70.3 1.2 slice_bitcast_fusion.1
  71.5 0.9 copy.37
  72.4 0.9 copy.46
  73.3 8.7 %all-to-all-done = bf16[4,2,39936]{2,1,0:T(2,128)(2,1)} async-done(((bf16[4,2,39936]{2,1,0:T(2,128)(2,1)}), bf16[4,2,39936]{2,1,0:T(2,128)(2,1)}, u32[]{:S(2)}, u32[]{:S(2)}) %all-to-all-start) | async-done | bytes 639008 | tf_op jit(solution)/shard_map/all_to_all | solution.py:57
  82.0 5.6 %reshape.66 = bf16[104,2,2,4,8,24]{5,4,3,2,1,0:T(8,128)(2,1)S(1)} reshape(bf16[4,2,39936]{2,1,0:T(2,128)(2,1)} %all-to-all-done) | data formatting | bytes 1277952
  87.6 4.4 %copy.86 = bf16[2,2,4,24,8,4,26]{3,5,4,6,2,1,0:T(4,128)(2,1)S(1)} copy(bf16[2,2,4,24,8,4,26]{3,4,2,1,0,6,5:T(8,128)(2,1)S(1)} %bitcast.166) | data formatting | bytes 1277952 | tf_op jit(solution)/shard_map/all_to_all | solution.py:57
  92.0 1.2 fusion.181
  93.2 1.6 squeeze.18
  94.8 2.9 fusion.16
  97.7 0.9 squeeze.19
  98.6 0.8 fusion.12
  99.3 2.0 convolution_subtract_fusion
  101.4 2.2 add_reduce_fusion
  103.8 0.3 copy.49
  104.1 18.8 %all_to_all.47 = f32[2,32,1248]{2,0,1:T(2,128)S(1)} all-to-all(f32[2,32,1248]{2,0,1:T(2,128)S(1)} %copy.49), channel_id=1, replica_groups=mesh['tm'=32,'slab'=4] {'tm'}, dimensions={1} | all-to-all | bytes 638976 | tf_op jit(solution)/shard_map/all_to_all | solution.py:71
  123.1 1.0 fusion.182
  124.4 193.9 %all-gather.3.cloned.1.call-done = f32[8192,64]{1,0:T(8,128)} async-done(((f32[64,64]{1,0:T(8,128)}), f32[8192,64]{1,0:T(8,128)}) %all-gather.3.cloned.1.call-update) | async-done | bytes 2097168 | tf_op jit(solution)/shard_map/all_gather | solution.py:72
  318.3 2.5 reduce_sum.29
  321.3 2.9 cholesky.89
  324.3 0.6 compare_reduce_fusion.4
  324.9 0.7 fusion.70
  325.6 2.4 custom-call.9
  328.0 0.3 fusion.87
  328.8 2.9 cholesky.100
  331.8 0.6 compare_reduce_fusion.3
  332.4 0.7 fusion.71
  333.1 2.4 custom-call.10
  335.5 0.2 fusion.84
  336.3 2.9 cholesky.111
  339.3 0.6 compare_reduce_fusion.2
  339.9 0.7 fusion.72
  340.6 2.4 custom-call.11
  343.0 0.2 fusion.81
  343.8 2.9 cholesky.122
  346.8 0.6 compare_reduce_fusion.1
  347.4 0.7 fusion.73
  348.1 2.4 custom-call.12
  350.5 0.2 fusion.78
  351.3 2.9 cholesky.133
  354.3 0.6 compare_reduce_fusion
  354.9 0.7 fusion.74
  355.6 2.4 custom-call.13
  358.0 0.2 fusion.75
  358.4 0.2 fusion.196
  358.6 0.4 fusion.36
  359.1 0.3 copy.56
  359.3 15.2 %all_to_all.48 = f32[32,2,1248]{2,1,0:T(2,128)S(1)} all-to-all(f32[32,2,1248]{2,1,0:T(2,128)S(1)} %copy.56), channel_id=1, replica_groups=mesh['tm'=32,'slab'=4] {'tm'}, dimensions={0} | all-to-all | bytes 638976 | tf_op jit(solution)/shard_map/all_to_all | solution.py:80
  374.6 0.3 reshape.37
  374.9 1.0 copy.58
  (50 shorter events, 3.6 us)
Async XLA Ops:
  39.6 4.3 %copy-start = (bf16[2,4,24,96,104]{4,3,2,1,0:T(8,128)(2,1)S(1)}, bf16[2,4,24,96,104]{4,3,2,1,0:T(8,128)(2,1)}, u32[]{:S(2)}) copy-start(bf16[2,4,24,96,104]{4,3,2,1,0:T(8,128)(2,1)} %squeeze.17) | copy-start | bytes 11501572
  43.8 5.1 %slice-start = ((s8[4718592]{0:T(1024)(128)(4,1)}), s8[4194304]{0:T(1024)(128)(4,1)S(1)}, s32[]{:S(2)}) async-start(s8[4718592]{0:T(1024)(128)(4,1)} %bitcast.162), calls=%async_computation.4 | async-start | bytes 8388608
  45.9 3.1 slice-start.1
  65.9 16.1 %all-to-all-start = ((bf16[4,2,39936]{2,1,0:T(2,128)(2,1)}), bf16[4,2,39936]{2,1,0:T(2,128)(2,1)}, u32[]{:S(2)}, u32[]{:S(2)}) async-start(bf16[4,2,39936]{2,1,0:T(2,128)(2,1)} %reshape.65), calls=%async_computation | async-start | bytes 1277952 | tf_op jit(solution)/shard_map/all_to_all | solution.py:57
  70.3 248.0 %all-gather.3.cloned.1.call-start = ((), (), s32[]{:S(2)}) async-start(), calls=%async_computation.3 | async-start | bytes 4227072 | tf_op jit(solution)/shard_map/all_gather | solution.py:72
  94.8 6.6 %copy-start.1 = (bf16[2,4,96,8,26]{2,3,4,1,0:T(8,128)(2,1)S(1)}, bf16[2,4,96,8,26]{2,3,4,1,0:T(8,128)(2,1)}, u32[]{:S(2)}) copy-start(bf16[2,4,96,8,26]{2,3,4,1,0:T(8,128)(2,1)} %squeeze.18) | copy-start | bytes 958468
  94.8 6.6 %copy-start.2 = (f32[4,8,26,96]{3,2,1,0:T(8,128)S(1)}, f32[4,8,26,96]{3,2,1,0:T(8,128)}, u32[]{:S(2)}) copy-start(f32[4,8,26,96]{3,2,1,0:T(8,128)} %copy.37) | copy-start | bytes 958468
Sparse Core Ops, SparseCore 0:
  124.3 193.9 all-gather.2
